TPU v7x, 32 devices: a whole 2x2x4 slice. The times are simulated.
32 devices in a mesh: rep: 4 (over y, x), table: 8 (over z, core).
Axes of the slice: x: 2, y: 2, z: 4, core: 2. Of those that a mesh axis runs over, the one named last changes fastest.
Arguments:
- cold_table: float32 [8192, 400], P('table'), may hold values from -3 to 3
- cold_state: float32 [8192], P('table'), may hold values from 0.05 to 1
- hot_table: float32 [1024, 400], P('table'), may hold values from -3 to 3
- hot_state: float32 [1024], P('table'), may hold values from 0.05 to 1
- relations: float32 [512, 400], replicated, may hold values from -2.5 to 2.5
- head_owner: int32 [16384, 1], P(('rep', 'table')), may hold values from 0 to 7; in each aligned block of 512 rows (0 to 511, 512 to 1023, ...) at most 128 rows name the same one
- head_row: int32 [16384], P(('rep', 'table')), may hold values from 0 to 1023
- edge_rel: int32 [16384], P(('rep', 'table')), may hold values from 0 to 511
- edge_tail: int32 [16384], P(('rep', 'table')), may hold values from 0 to 1023, as said below
- neg_ids: int32 [4, 64], P('rep', 'table'), may hold values from 0 to 1023
Outputs:
- new_cold_table: float32 [8192, 400], P('table')
- new_cold_state: float32 [8192], P('table')
- new_hot_table: float32 [1024, 400], P('table')
- new_hot_state: float32 [1024], P('table')
Inputs may be any that keep to these rules, and one draw needn't show every extreme that they name: `head_owner`: among the edges of one device (aligned blocks of 512), no owner is named more than 128 times. `neg_ids`: column j names a row of the cold rows of table index j // 8. `edge_tail`: among the edges of one device (aligned blocks of 512), the tails that lie in one aligned block of 128 hot rows are at most 32 distinct rows, and in some such block exactly 32.
All inputs are finite; a program needn't handle non-finite values.
Results may differ from a plain program's by a relative error of at most 0.00045.
The roundings to bfloat16 on the way count: a program that leaves them out, or rounds other values in their place, can miss the bound.
Values may be sent and summed in bfloat16 or wider, within the bound.
A program may use at most 128 MiB of HBM per device.

v0:
```python
import jax
import jax.numpy as jnp
from jax import lax
from jax.sharding import PartitionSpec as P

learn_rate = 0.5


def with_relation(relation, vector):
    half_width = vector.shape[1] // 2
    v_re, v_im = (vector[:, :half_width], vector[:, half_width:])
    r_re, r_im = (relation[:, :half_width], relation[:, half_width:])
    return jnp.concatenate([v_re * r_re - v_im * r_im, v_re * r_im + v_im * r_re], axis=1)


def against_relation(relation, vector):
    half_width = vector.shape[1] // 2
    v_re, v_im = (vector[:, :half_width], vector[:, half_width:])
    r_re, r_im = (relation[:, :half_width], relation[:, half_width:])
    return jnp.concatenate([r_re * v_re + r_im * v_im, r_re * v_im - r_im * v_re], axis=1)


def edge_terms(head_vec, relation, tail_vec, negatives, live_mask):
    contract = (((1,), (1,)), ((), ()))
    across = (((0,), (0,)), ((), ()))
    head_f = head_vec.astype(jnp.float32)
    tail_f = tail_vec.astype(jnp.float32)
    queries = with_relation(relation, head_f)
    probes = against_relation(relation, tail_f)
    positive = jnp.sum(queries * tail_f, axis=1)
    query_b = queries.astype(jnp.bfloat16)
    probe_b = probes.astype(jnp.bfloat16)
    tail_scores = lax.dot_general(query_b, negatives, contract, preferred_element_type=jnp.float32)
    head_scores = lax.dot_general(probe_b, negatives, contract, preferred_element_type=jnp.float32)
    pos_weight = -jax.nn.sigmoid(-positive) * live_mask
    tail_weight = (jax.nn.sigmoid(tail_scores) * live_mask[:, None]).astype(jnp.bfloat16)
    head_weight = (jax.nn.sigmoid(head_scores) * live_mask[:, None]).astype(jnp.bfloat16)
    tail_mix = jnp.dot(tail_weight, negatives, preferred_element_type=jnp.float32)
    head_mix = jnp.dot(head_weight, negatives, preferred_element_type=jnp.float32)
    head_grad = against_relation(relation, pos_weight[:, None] * tail_f + tail_mix).astype(
        jnp.bfloat16
    )
    tail_grad = with_relation(relation, pos_weight[:, None] * head_f + head_mix)
    neg_grad = lax.dot_general(
        tail_weight, query_b, across, preferred_element_type=jnp.float32
    ) + lax.dot_general(head_weight, probe_b, across, preferred_element_type=jnp.float32)
    return (head_grad, tail_grad, neg_grad)


def adagrad(weights, state, grad):
    new_state = state + jnp.mean(grad * grad, axis=1)
    return (weights - learn_rate * grad / jnp.sqrt(new_state)[:, None], new_state)


def per_device(
    cold_table,
    cold_state,
    hot_table,
    hot_state,
    relations,
    head_owner,
    head_row,
    edge_rel,
    edge_tail,
    neg_ids,
):
    n_table = lax.axis_size("table")
    edge_count = head_row.shape[0]
    capacity = 2 * edge_count // n_table
    slot_total = n_table * capacity
    feature_width = cold_table.shape[1]
    cold_bf = cold_table.astype(jnp.bfloat16)
    hot_bf = hot_table.astype(jnp.bfloat16)
    local_negs = cold_bf[neg_ids[0]]
    hot_all, negatives = (
        lax.all_gather(hot_bf, "table", axis=0, tiled=True),
        lax.all_gather(local_negs, "table", axis=0, tiled=True),
    )
    owners = head_owner[:, 0]
    onehot = (owners[:, None] == jnp.arange(n_table, dtype=jnp.int32)[None, :]).astype(jnp.int32)
    slot_rank = jnp.sum((jnp.cumsum(onehot, axis=0) - onehot) * onehot, axis=1)
    slot_ids = owners * capacity + slot_rank
    cold_grad = jnp.zeros(cold_table.shape, jnp.float32)
    records = jnp.stack([head_row, edge_rel, edge_tail, jnp.ones_like(head_row)])
    packed = jnp.zeros((4, slot_total), jnp.int32).at[:, slot_ids].set(records)
    arrived = lax.all_to_all(
        packed.reshape(4, n_table, capacity), "table", split_axis=1, concat_axis=1, tiled=True
    )
    arrived = arrived.reshape(4, slot_total)
    row_ids, rel_ids, tail_ids, live_ids = (arrived[0], arrived[1], arrived[2], arrived[3])
    tail_live = live_ids.astype(jnp.float32)
    head_grad, tail_grad, neg_grad = edge_terms(
        cold_bf[row_ids], relations[rel_ids], hot_all[tail_ids], negatives, tail_live
    )
    cold_grad = cold_grad.at[row_ids].add(head_grad.astype(jnp.float32))
    hot_grad = jnp.zeros((hot_all.shape[0], feature_width), jnp.float32).at[tail_ids].add(tail_grad)
    hot_share, neg_share = (
        lax.psum_scatter(hot_grad, "table", scatter_dimension=0, tiled=True),
        lax.psum_scatter(neg_grad, "table", scatter_dimension=0, tiled=True),
    )
    cold_grad = cold_grad.at[neg_ids[0]].add(neg_share)
    cold_total, hot_total = lax.psum((cold_grad, hot_share), "rep")
    new_cold_table, new_cold_state = adagrad(cold_table, cold_state, cold_total)
    new_hot_table, new_hot_state = adagrad(hot_table, hot_state, hot_total)
    return (new_cold_table, new_cold_state, new_hot_table, new_hot_state)


def solution(mesh):
    in_specs = (
        P("table", None),
        P("table"),
        P("table", None),
        P("table"),
        P(),
        P(("rep", "table"), None),
        P(("rep", "table")),
        P(("rep", "table")),
        P(("rep", "table")),
        P("rep", "table"),
    )
    out_specs = (P("table", None), P("table"), P("table", None), P("table"))
    return jax.shard_map(
        per_device, mesh=mesh, in_specs=in_specs, out_specs=out_specs, check_vma=False
    )
```

profile of v0, /device:TPU:9, one launch (start us, length us, event | category | flops | bytes accessed | tf_op | source)
XLA Modules:
  0.0 253.4 jit_solution(18391554835723637068)
XLA Ops:
  11.9 1.8 scatter_custom_fusion
  14.5 5.6 %all-to-all-start = ((s32[4,8,128]{2,0,1:T(4,128)}), s32[4,8,128]{2,0,1:T(4,128)S(1)}, u32[]{:S(2)}, u32[]{:S(2)}) async-start(s32[4,8,128]{2,0,1:T(4,128)} %copy.56), calls=%async_computation | async-start | bytes 32768 | tf_op jit(solution)/shard_map/all_to_all | solution.py:86
  20.8 16.3 %all_gather.6 = bf16[1024,400]{0,1:T(8,128)(2,1)} all-gather(bf16[128,400]{0,1:T(8,128)(2,1)S(1)} %convert_element_type.50), channel_id=1, replica_groups=mesh['rep'=4,'table'=8] {'table'}, dimensions={0}, use_global_device_ids=true | all-gather | bytes 921600 | tf_op jit(solution)/shard_map/all_gather | solution.py:76
  37.1 1.9 copy.69
  40.4 1.7 convert_element_type.48
  44.2 12.6 %all-gather = bf16[64,400]{1,0:T(8,128)(2,1)S(1)} all-gather(bf16[8,400]{1,0:T(8,128)(2,1)S(1)} %gather_fusion.3), channel_id=2, replica_groups=mesh['rep'=4,'table'=8] {'table'}, dimensions={0}, use_global_device_ids=true | all-gather | bytes 57600 | tf_op jit(solution)/shard_map/all_gather | solution.py:77
  56.9 4.9 %gather_fusion = f32[1024,400]{1,0:T(8,128)} fusion(f32[512,400]{1,0:T(8,128)S(1)} %copy.59, s32[1024]{0:T(1024)S(1)} %broadcast_clamp_fusion.2), kind=kCustom, calls=%fused_computation | custom fusion | bytes 3280896 | tf_op jit(solution)/shard_map/gather | solution.py:93
  61.8 3.4 %fusion.30 = (f32[1024,200]{1,0:T(8,128)}, f32[1024,200]{1,0:T(8,128)}) fusion(f32[1024,400]{1,0:T(8,128)} %gather_fusion), kind=kLoop, calls=%fused_computation.79 | loop fusion | bytes 3276800 | tf_op jit(solution)/shard_map/slice | solution.py:19
  66.7 2.4 copy.76
  69.2 5.1 %gather_fusion.2 = bf16[1024,400]{1,0:T(8,128)(2,1)} fusion(bf16[1024,400]{1,0:T(8,128)(2,1)S(1)} %copy.65, s32[1024]{0:T(1024)S(1)} %broadcast_clamp_fusion), kind=kCustom, calls=%fused_computation.2 | custom fusion | bytes 1642496 | tf_op jit(solution)/shard_map/gather | solution.py:93
  77.0 5.1 %gather_fusion.1 = bf16[1024,400]{1,0:T(8,128)(2,1)} fusion(bf16[1024,400]{1,0:T(8,128)(2,1)S(1)} %convert_element_type.48, s32[1024]{0:T(1024)S(1)} %broadcast_clamp_fusion.1), kind=kCustom, calls=%fused_computation.1 | custom fusion | bytes 1642496 | tf_op jit(solution)/shard_map/gather | solution.py:93
  82.1 2.2 copy.62
  87.9 1.6 multiply_add_fusion.1
  93.5 2.5 multiply_subtract_fusion
  96.1 1.8 copy.70
  97.9 9.4 %scatter_custom_fusion.3 = f32[1024,400]{1,0:T(8,128)} fusion(s32[1024]{0:T(1024)S(1)} %bitcast.65, f32[1024,400]{1,0:T(8,128)} %copy.70, f32[]{:T(128)} %constant.9.clone.1), kind=kCustom, calls=%fused_computation.29 | custom fusion | flops 409600 | bytes 1638912 | tf_op jit(solution)/shard_map/scatter-add | solution.py:96
  107.6 1.8 copy.68
  109.4 8.5 %scatter_custom_fusion.1 = f32[1024,400]{1,0:T(8,128)S(1)} fusion(s32[1024]{0:T(1024)S(1)} %bitcast.63, f32[1024,400]{1,0:T(8,128)} %copy.68, f32[]{:T(128)} %constant.9.clone.1), kind=kCustom, calls=%fused_computation.31 | custom fusion | flops 409600 | bytes 1638912 | tf_op jit(solution)/shard_map/scatter-add | solution.py:95
  117.9 1.6 scatter_fusion
  119.6 35.5 %reduce-scatter.5.cloned.1.call-done = f32[128,400]{1,0:T(8,128)} async-done(((f32[1024,400]{1,0:T(8,128)}), f32[128,400]{1,0:T(8,128)}) %reduce-scatter.5.cloned.1.call-update) | async-done | bytes 204816 | tf_op jit(solution)/shard_map/reduce_scatter | solution.py:98
  155.2 81.6 %all-reduce.3.cloned.1.call-done = (f32[1024,400]{1,0:T(8,128)}, f32[128,400]{1,0:T(8,128)}) async-done(((f32[1024,400]{1,0:T(8,128)}, f32[128,400]{1,0:T(8,128)}), (f32[1024,400]{1,0:T(8,128)}, f32[128,400]{1,0:T(8,128)})) %all-reduce.3.cloned.1.call-update) | async-done | bytes 1843216 | tf_op jit(solution)/shard_map/psum | solution.py:102
  236.8 1.8 multiply_reduce_fusion
  239.2 3.3 %divide_subtract_fusion = f32[1024,400]{1,0:T(8,128)} fusion(f32[1024,400]{1,0:T(8,128)S(1)} %copy-done, f32[1024,400]{1,0:T(8,128)} %get-tuple-element.16, f32[1024]{0:T(1024)S(1)} %get-tuple-element.20), kind=kLoop, calls=%fused_computation.8 | loop fusion | flops 1228800 | bytes 4919296 | tf_op jit(solution)/shard_map/sub | solution.py:52
  242.6 2.8 %copy.72 = f32[1024,400]{0,1:T(8,128)} copy(f32[1024,400]{1,0:T(8,128)} %divide_subtract_fusion) | data formatting | bytes 3276800
  (71 shorter events, 24.2 us)
Async XLA Ops:
  7.2 13.6 %copy-start.7 = (f32[128,400]{0,1:T(8,128)S(1)}, f32[128,400]{0,1:T(8,128)}, u32[]{:S(2)}) copy-start(f32[128,400]{0,1:T(8,128)} %param.12) | copy-start | bytes 614404
  7.2 29.9 %copy-start.5 = (f32[1024,400]{0,1:T(8,128)S(1)}, f32[1024,400]{0,1:T(8,128)}, u32[]{:S(2)}) copy-start(f32[1024,400]{0,1:T(8,128)} %param.10) | copy-start | bytes 4915204
  14.5 42.3 %all-to-all-start = ((s32[4,8,128]{2,0,1:T(4,128)}), s32[4,8,128]{2,0,1:T(4,128)S(1)}, u32[]{:S(2)}, u32[]{:S(2)}) async-start(s32[4,8,128]{2,0,1:T(4,128)} %copy.56), calls=%async_computation | async-start | bytes 32768 | tf_op jit(solution)/shard_map/all_to_all | solution.py:86
  20.1 97.8 %reduce-scatter.3.cloned.1.call-start = ((), (), s32[]{:S(2)}) async-start(), calls=%async_computation.3 | async-start | bytes 147456 | tf_op jit(solution)/shard_map/reduce_scatter | solution.py:99
  84.3 1.5 copy-start.2
  84.3 1.9 copy-start.4
  89.5 1.1 copy-start.3
  93.3 61.8 %reduce-scatter.5.cloned.1.call-start = ((), (), s32[]{:S(2)}) async-start(), calls=%async_computation.4 | async-start | bytes 2359296 | tf_op jit(solution)/shard_map/reduce_scatter | solution.py:98
  107.3 129.5 %all-reduce.3.cloned.1.call-start = ((), (), s32[]{:S(2)}) async-start(), calls=%async_computation.5 | async-start | bytes 4718592 | tf_op jit(solution)/shard_map/psum | solution.py:102
  119.5 35.5 %copy-start.1 = (f32[1024,400]{1,0:T(8,128)}, f32[1024,400]{1,0:T(8,128)S(1)}, u32[]{:S(2)}) copy-start(f32[1024,400]{1,0:T(8,128)S(1)} %scatter_fusion) | copy-start | bytes 4915204
  155.1 83.6 %copy-start.8 = (f32[1024]{0:T(1024)S(1)}, f32[1024]{0:T(1024)}, u32[]{:S(2)}) copy-start(f32[1024]{0:T(1024)} %param.11) | copy-start | bytes 12292
  155.1 84.1 %copy-start = (f32[1024,400]{1,0:T(8,128)S(1)}, f32[1024,400]{1,0:T(8,128)}, u32[]{:S(2)}) copy-start(f32[1024,400]{1,0:T(8,128)} %copy.69) | copy-start | bytes 4915204
  242.6 2.8 %copy-start.6 = (f32[128,400]{1,0:T(8,128)S(1)}, f32[128,400]{1,0:T(8,128)}, u32[]{:S(2)}) copy-start(f32[128,400]{1,0:T(8,128)} %get-tuple-element.17) | copy-start | bytes 614404
  242.6 2.9 %copy-start.9 = (f32[128]{0:T(128)S(1)}, f32[128]{0:T(128)}, u32[]{:S(2)}) copy-start(f32[128]{0:T(128)} %param.13) | copy-start | bytes 1540
Sparse Core Ops, SparseCore 0:
  93.4 23.9 reduce-scatter.2
  119.8 35.1 reduce-scatter.4
  158.5 78.2 all-reduce.2
where the time goes:
time: 256 us; the launch traced here: 253 us
  waiting for transfers between devices  117 us (46%)
  local copies, waits for them, and re-layouts  43.2 us (17%)
  other arithmetic  39.1 us (15%)
  blocking collectives  28.9 us (11%)
  between operations  14 us (5%)
  starting transfers between devices  5.9 us (2%)
  matrix products  5.16 us (2%)
    psum x1, waiting for transfers between devices, per_device(): cold_total, hot_total = lax.psum((cold_grad, hot_share), 'rep')  81.6 us
    reduce_scatter x1, waiting for transfers between devices, per_device(): lax.psum_scatter(hot_grad, 'table', scatter_dimension=0, tiled=True)  35.5 us
    all_gather x1, blocking collectives, per_device(): lax.all_gather(hot_bf, 'table', axis=0, tiled=True)  16.3 us
    all_gather x1, blocking collectives, per_device(): lax.all_gather(local_negs, 'table', axis=0, tiled=True)  12.6 us
    unnamed x27, local copies, waits for them, and re-layouts  12.3 us
    scatter-add x1, other arithmetic, per_device(): jnp.zeros((hot_all.shape[0], feature_width), jnp.float32).at[tail_ids]  9.36 us
    scatter-add x1, other arithmetic, per_device(): cold_grad = cold_grad.at[row_ids].add(head_grad.astype(jnp.float32))  8.49 us
    gather x2, local copies, waits for them, and re-layouts, per_device(): cold_bf[row_ids]  7.28 us
  transfers between devices with their start and end apart: 4, of which 2 were waited for; matrix products, arithmetic and copies ran while one was open for 13% of the time, Pallas kernels for 0%

commit v1 on v0

--- a/solution.py
+++ b/solution.py
@@ -1,6 +1,10 @@
+import functools
+
 import jax
 import jax.numpy as jnp
 from jax import lax
+from jax.experimental import pallas as pl
+from jax.experimental.pallas import tpu as pltpu
 from jax.sharding import PartitionSpec as P
 
 learn_rate = 0.5
@@ -78,7 +82,10 @@
     )
     owners = head_owner[:, 0]
     onehot = (owners[:, None] == jnp.arange(n_table, dtype=jnp.int32)[None, :]).astype(jnp.int32)
-    slot_rank = jnp.sum((jnp.cumsum(onehot, axis=0) - onehot) * onehot, axis=1)
+    position = jnp.arange(edge_count)
+    before = (position[:, None] > position[None, :]).astype(jnp.bfloat16)
+    counts = jnp.dot(before, onehot.astype(jnp.bfloat16), preferred_element_type=jnp.float32)
+    slot_rank = jnp.sum(counts.astype(jnp.int32) * onehot, axis=1)
     slot_ids = owners * capacity + slot_rank
     cold_grad = jnp.zeros(cold_table.shape, jnp.float32)
     records = jnp.stack([head_row, edge_rel, edge_tail, jnp.ones_like(head_row)])
@@ -103,6 +110,445 @@
     new_cold_table, new_cold_state = adagrad(cold_table, cold_state, cold_total)
     new_hot_table, new_hot_state = adagrad(hot_table, hot_state, hot_total)
     return (new_cold_table, new_cold_state, new_hot_table, new_hot_state)
+
+
+def fits_kernel(n_rep, n_table, cold_rows, hot_rows, edges, neg_dev, width, rel_count):
+    quarter = hot_rows // n_rep
+    sizes = (n_rep, n_table, cold_rows, hot_rows, edges)
+    return (
+        all(s & (s - 1) == 0 for s in sizes)
+        and 2 * edges // n_table == 128
+        and n_table % 2 == 0
+        and quarter % 16 == 0
+        and quarter <= 256
+        and neg_dev == 8
+        and cold_rows % 128 == 0
+        and cold_rows <= 4096
+        and width % 2 == 0
+        and width <= 512
+        and n_table * hot_rows <= 4096
+        and rel_count <= 1024
+    )
+
+
+def edge_kernel(
+    dims,
+    cold_ref,
+    cstate_ref,
+    hot_ref,
+    hstate_ref,
+    rel_ref,
+    owner_ref,
+    hrow_ref,
+    erel_ref,
+    etail_ref,
+    nid_ref,
+    cold_out,
+    cstate_out,
+    hot_out,
+    hstate_out,
+    coldbf,
+    relparts,
+    outbox,
+    ids,
+    hotall,
+    negall,
+    negbf,
+    nidall,
+    rowids,
+    hgrad,
+    hotgrad,
+    hotrecv,
+    hotsum,
+    hotrecv2,
+    hotfin,
+    neggrad,
+    negrecv,
+    negfin,
+    send1,
+    recv1,
+    send2,
+    recv2,
+    send3,
+    recv3,
+    send4,
+    recv4,
+    send5,
+    recv5,
+    send6,
+    recv6,
+    send7,
+    recv7,
+):
+    n_rep, n_table = dims
+    f32, bf16, i32 = jnp.float32, jnp.bfloat16, jnp.int32
+    rep, tab = lax.axis_index("rep"), lax.axis_index("table")
+    rows_c, width = cold_ref.shape
+    half = width // 2
+    edges = owner_ref.shape[0]
+    rows_h = hot_ref.shape[0]
+    quarter = rows_h // n_rep
+    hot_total = n_table * rows_h
+    rel_count = rel_ref.shape[0]
+    padw = 256
+    full = 2 * padw
+
+    def spread(v):
+        pad = jnp.zeros((v.shape[0], padw - half), v.dtype)
+        return jnp.concatenate([v[:, :half], pad, v[:, half:], pad], axis=1)
+
+    def close(v):
+        return jnp.concatenate([v[:, :half], v[:, padw : padw + half]], axis=1)
+
+    def dot(a, b, ca=1, cb=0):
+        return lax.dot_general(a, b, (((ca,), (cb,)), ((), ())), preferred_element_type=f32)
+
+    def hot_one(cond):
+        return jnp.where(cond, 1.0, 0.0).astype(bf16)
+
+    def to_table(step):
+        return (rep, lax.rem(tab + step, n_table))
+
+    def to_rep(step):
+        return (lax.rem(rep + step, n_rep), tab)
+
+    def remote(src, dst, ss, rs, dev):
+        return pltpu.make_async_remote_copy(
+            src_ref=src,
+            dst_ref=dst,
+            send_sem=ss,
+            recv_sem=rs,
+            device_id=dev,
+            device_id_type=pl.DeviceIdType.MESH,
+        )
+
+    barrier = pltpu.get_barrier_semaphore()
+    for s in range(1, n_table):
+        pl.semaphore_signal(barrier, 1, device_id=to_table(s), device_id_type=pl.DeviceIdType.MESH)
+    for s in range(1, n_rep):
+        pl.semaphore_signal(barrier, 1, device_id=to_rep(s), device_id_type=pl.DeviceIdType.MESH)
+
+    mine = hot_ref[pl.ds(pl.multiple_of(rep * quarter, quarter), quarter), :]
+    hotall[rep, tab] = spread(mine).astype(bf16)
+
+    owner = owner_ref[...]
+    lane = lax.broadcasted_iota(i32, (edges, 128), 1)
+    owned = lane == owner
+    owned_b = hot_one(owned)
+    before = hot_one(
+        lax.broadcasted_iota(i32, (edges, edges), 0) > lax.broadcasted_iota(i32, (edges, edges), 1)
+    )
+    rank = jnp.sum(jnp.where(owned, dot(before, owned_b), 0.0), axis=1, keepdims=True)
+    slot = owner * 128 + rank.astype(i32)
+    hrow, erel, etail = hrow_ref[...], erel_ref[...], etail_ref[...]
+    t_block = etail // rows_h
+    t_in = etail % rows_h
+    t_group = (t_in // quarter) * n_table + t_block
+    fields = [
+        hrow // 32,
+        hrow % 32,
+        erel // 32,
+        erel % 32,
+        t_group,
+        t_in % quarter,
+        jnp.ones_like(hrow),
+        jnp.zeros_like(hrow),
+    ]
+    records = jnp.concatenate([f.astype(f32) for f in fields], axis=0).astype(bf16)
+    for o in range(n_table):
+        place = hot_one(lane + o * 128 == slot)
+        outbox[o] = dot(records, place)
+    pl.semaphore_wait(barrier, n_table + n_rep - 2)
+    ids[rep, tab] = outbox[tab]
+
+    first = []
+    for s in range(1, n_table):
+        dev = to_table(s)
+        first.append(remote(outbox.at[dev[1]], ids.at[rep, tab], send1.at[0, s], recv1.at[0, s], dev))
+        first.append(remote(hotall.at[rep, tab], hotall.at[rep, tab], send1.at[1, s], recv1.at[1, s], dev))
+    for c in first:
+        c.start()
+
+    coldbf[...] = spread(cold_ref[...]).astype(bf16)
+    nid = nid_ref[...]
+    pick = hot_one(lax.broadcasted_iota(i32, (8, rows_c), 1) == nid)
+    negall[rep, tab] = dot(pick, coldbf[...])
+    nidall[rep] = jnp.broadcast_to(nid.astype(f32), (8, 128))
+    more = []
+    for s in range(1, n_table):
+        more.append(
+            remote(negall.at[rep, tab], negall.at[rep, tab], send1.at[2, s], recv1.at[2, s], to_table(s))
+        )
+    for c in more:
+        c.start()
+
+    rel = spread(rel_ref[...])
+    rel_a = rel.astype(bf16)
+    rest = rel - rel_a.astype(f32)
+    rel_b = rest.astype(bf16)
+    relparts[0] = rel_a
+    relparts[1] = rel_b
+    relparts[2] = (rest - rel_b.astype(f32)).astype(bf16)
+    hotgrad[...] = jnp.zeros_like(hotgrad)
+    neggrad[...] = jnp.zeros_like(neggrad)
+
+    for c in first + more:
+        c.wait()
+
+    second = []
+    for s in range(1, n_rep):
+        dev = to_rep(s)
+        second.append(remote(hotall.at[rep], hotall.at[rep], send2.at[0, s], recv2.at[0, s], dev))
+        second.append(remote(ids.at[rep], ids.at[rep], send2.at[1, s], recv2.at[1, s], dev))
+        second.append(remote(negall.at[rep], negall.at[rep], send2.at[2, s], recv2.at[2, s], dev))
+        second.append(remote(nidall.at[rep], nidall.at[rep], send2.at[3, s], recv2.at[3, s], dev))
+    for c in second:
+        c.start()
+    for c in second:
+        c.wait()
+    negbf[...] = negall[...].reshape(n_rep, n_table * 8, full).astype(bf16)
+
+    def with_rel(r, v):
+        r_re, r_im, v_re, v_im = r[:, :padw], r[:, padw:], v[:, :padw], v[:, padw:]
+        return jnp.concatenate([v_re * r_re - v_im * r_im, v_re * r_im + v_im * r_re], axis=1)
+
+    def against_rel(r, v):
+        r_re, r_im, v_re, v_im = r[:, :padw], r[:, padw:], v[:, :padw], v[:, padw:]
+        return jnp.concatenate([r_re * v_re + r_im * v_im, r_re * v_im - r_im * v_re], axis=1)
+
+    chunk = 256
+    per = n_table * 128 // chunk
+
+    def edges_of(q, own):
+        def body(c, carry):
+            f = jnp.concatenate([ids[q, 2 * c], ids[q, 2 * c + 1]], axis=1)
+            g = f.T.astype(i32)
+            f = f.astype(i32)
+            row_row = f[0:1] * 32 + f[1:2]
+            rowids[q, c] = row_row
+            row_col = g[:, 0:1] * 32 + g[:, 1:2]
+            rel_col = g[:, 2:3] * 32 + g[:, 3:4]
+            tail_col = g[:, 4:5] * quarter + g[:, 5:6]
+            live = g[:, 6:7].astype(f32)
+            wide = lambda n: lax.broadcasted_iota(i32, (chunk, n), 1)
+            head_v = dot(hot_one(wide(rows_c) == row_col), coldbf[...])
+            tail_v = dot(hot_one(wide(hot_total) == tail_col), hotall[...].reshape(hot_total, full))
+            pick_r = hot_one(wide(rel_count) == rel_col)
+            r = dot(pick_r, relparts[0]) + dot(pick_r, relparts[1]) + dot(pick_r, relparts[2])
+            neg = negbf[q]
+            queries = with_rel(r, head_v)
+            positive = jnp.sum(queries * tail_v, axis=1, keepdims=True)
+            query_b = queries.astype(bf16)
+            tail_w = (jax.nn.sigmoid(dot(query_b, neg, 1, 1)) * live).astype(bf16)
+            pos_w = -jax.nn.sigmoid(-positive) * live
+            hgrad[q, c] = against_rel(r, pos_w * tail_v + dot(tail_w, neg)).astype(bf16)
+            if own:
+                probe_b = against_rel(r, tail_v).astype(bf16)
+                head_w = (jax.nn.sigmoid(dot(probe_b, neg, 1, 1)) * live).astype(bf16)
+                tail_g = with_rel(r, pos_w * head_v + dot(head_w, neg))
+                neg_g = dot(tail_w, query_b, 0, 0) + dot(head_w, probe_b, 0, 0)
+                neggrad[...] += neg_g.reshape(n_table, 8, full)
+                hi = tail_g.astype(bf16)
+                lo = (tail_g - hi.astype(f32)).astype(bf16)
+                tail_row = f[4:5] * quarter + f[5:6]
+                put = hot_one(lax.broadcasted_iota(i32, (hot_total, chunk), 0) == tail_row)
+                hotgrad[...] += (dot(put, hi) + dot(put, lo)).reshape(hotgrad.shape)
+            return carry
+
+        lax.fori_loop(0, per, body, 0)
+
+    edges_of(rep, True)
+
+    third = []
+    for s in range(1, n_rep):
+        dev = to_rep(s)
+        third.append(remote(hotgrad.at[dev[0]], hotrecv.at[rep], send3.at[s], recv3.at[s], dev))
+    for s in range(1, n_table):
+        dev = to_table(s)
+        third.append(remote(neggrad.at[dev[1]], negrecv.at[tab], send6.at[s], recv6.at[s], dev))
+    for c in third:
+        c.start()
+    hotrecv[rep] = hotgrad[rep]
+    negrecv[tab] = neggrad[tab]
+
+    others = [lax.rem(rep + s, n_rep) for s in range(1, n_rep)]
+    split = max(1, len(others) // 3)
+    for q in others[:split]:
+        edges_of(q, False)
+
+    for c in third:
+        c.wait()
+    acc = hotrecv[0]
+    for k in range(1, n_rep):
+        acc = acc + hotrecv[k]
+    hotsum[...] = acc
+    nacc = negrecv[0]
+    for k in range(1, n_table):
+        nacc = nacc + negrecv[k]
+    negfin[rep] = nacc
+    fourth = []
+    for s in range(1, n_table):
+        dev = to_table(s)
+        fourth.append(remote(hotsum.at[dev[1]], hotrecv2.at[tab], send4.at[s], recv4.at[s], dev))
+    for s in range(1, n_rep):
+        fourth.append(remote(negfin.at[rep], negfin.at[rep], send7.at[s], recv7.at[s], to_rep(s)))
+    for c in fourth:
+        c.start()
+    hotrecv2[tab] = hotsum[tab]
+
+    for q in others[split : 2 * split]:
+        edges_of(q, False)
+
+    for c in fourth:
+        c.wait()
+    acc = hotrecv2[0]
+    for k in range(1, n_table):
+        acc = acc + hotrecv2[k]
+    hotfin[rep] = acc
+    fifth = [remote(hotfin.at[rep], hotfin.at[rep], send5.at[s], recv5.at[s], to_rep(s)) for s in range(1, n_rep)]
+    for c in fifth:
+        c.start()
+
+    for q in others[2 * split :]:
+        edges_of(q, False)
+
+    def step(weights, state, grad):
+        new_state = state + jnp.sum(grad * grad, axis=1, keepdims=True) / width
+        return weights - learn_rate * close(grad) / jnp.sqrt(new_state), new_state
+
+    neg_total = negfin[...].reshape(n_rep * 8, full)
+    neg_hi = neg_total.astype(bf16)
+    neg_rest = neg_total - neg_hi.astype(f32)
+    neg_mid = neg_rest.astype(bf16)
+    neg_lo = (neg_rest - neg_mid.astype(f32)).astype(bf16)
+    neg_col = nidall[...].reshape(n_rep * 8, 128).astype(i32)
+    block = 128
+
+    def finish(b, carry):
+        start = pl.multiple_of(b * block, block)
+        base = lax.broadcasted_iota(i32, (block, chunk), 0) + start
+        grad = jnp.zeros((block, full), f32)
+        for q in range(n_rep):
+            for c in range(per):
+                grad = grad + dot(hot_one(base == rowids[q, c]), hgrad[q, c])
+        put = hot_one(lax.broadcasted_iota(i32, (n_rep * 8, block), 1) + start == neg_col)
+        grad = grad + (dot(put, neg_hi, 0, 0) + dot(put, neg_mid, 0, 0) + dot(put, neg_lo, 0, 0))
+        at = pl.ds(start, block)
+        table, state = step(cold_ref[at, :], cstate_ref[at, :], grad)
+        cold_out[at, :] = table
+        cstate_out[at, :] = state
+        return carry
+
+    lax.fori_loop(0, rows_c // block, finish, 0)
+
+    for c in fifth:
+        c.wait()
+    table, state = step(hot_ref[...], hstate_ref[...], hotfin[...].reshape(rows_h, full))
+    hot_out[...] = table
+    hstate_out[...] = state
+
+
+def per_device_kernel(
+    cold_table,
+    cold_state,
+    hot_table,
+    hot_state,
+    relations,
+    head_owner,
+    head_row,
+    edge_rel,
+    edge_tail,
+    neg_ids,
+):
+    n_rep, n_table = lax.axis_size("rep"), lax.axis_size("table")
+    rows_c, width = cold_table.shape
+    rows_h = hot_table.shape[0]
+    edges = head_row.shape[0]
+    rel_count = relations.shape[0]
+    quarter = rows_h // n_rep
+    full, chunk = 512, 256
+    per = n_table * 128 // chunk
+    f32, bf16 = jnp.float32, jnp.bfloat16
+    dma = pltpu.SemaphoreType.DMA
+    vmem = pl.BlockSpec(memory_space=pltpu.VMEM)
+    outs = pl.pallas_call(
+        functools.partial(edge_kernel, (n_rep, n_table)),
+        out_shape=[
+            jax.ShapeDtypeStruct((rows_c, width), f32),
+            jax.ShapeDtypeStruct((rows_c, 1), f32),
+            jax.ShapeDtypeStruct((rows_h, width), f32),
+            jax.ShapeDtypeStruct((rows_h, 1), f32),
+        ],
+        in_specs=[vmem] * 10,
+        out_specs=[vmem] * 4,
+        scratch_shapes=[
+            pltpu.VMEM((rows_c, full), bf16),
+            pltpu.VMEM((3, rel_count, full), bf16),
+            pltpu.VMEM((n_table, 8, 128), f32),
+            pltpu.VMEM((n_rep, n_table, 8, 128), f32),
+            pltpu.VMEM((n_rep, n_table, quarter, full), bf16),
+            pltpu.VMEM((n_rep, n_table, 8, full), f32),
+            pltpu.VMEM((n_rep, n_table * 8, full), bf16),
+            pltpu.VMEM((n_rep, 8, 128), f32),
+            pltpu.VMEM((n_rep, per, 1, chunk), jnp.int32),
+            pltpu.VMEM((n_rep, per, chunk, full), bf16),
+            pltpu.VMEM((n_rep, n_table, quarter, full), f32),
+            pltpu.VMEM((n_rep, n_table, quarter, full), f32),
+            pltpu.VMEM((n_table, quarter, full), f32),
+            pltpu.VMEM((n_table, quarter, full), f32),
+            pltpu.VMEM((n_rep, quarter, full), f32),
+            pltpu.VMEM((n_table, 8, full), f32),
+            pltpu.VMEM((n_table, 8, full), f32),
+            pltpu.VMEM((n_rep, 8, full), f32),
+            dma((3, n_table)),
+            dma((3, n_table)),
+            dma((4, n_rep)),
+            dma((4, n_rep)),
+            dma((n_rep,)),
+            dma((n_rep,)),
+            dma((n_table,)),
+            dma((n_table,)),
+            dma((n_rep,)),
+            dma((n_rep,)),
+            dma((n_table,)),
+            dma((n_table,)),
+            dma((n_rep,)),
+            dma((n_rep,)),
+        ],
+        compiler_params=pltpu.CompilerParams(
+            collective_id=0, has_side_effects=True, vmem_limit_bytes=56 * 1024 * 1024
+        ),
+        name="edge_window",
+    )(
+        cold_table,
+        cold_state[:, None],
+        hot_table,
+        hot_state[:, None],
+        relations,
+        head_owner,
+        head_row[None, :],
+        edge_rel[None, :],
+        edge_tail[None, :],
+        neg_ids.reshape(-1, 1),
+    )
+    return (outs[0], outs[1][:, 0], outs[2], outs[3][:, 0])
+
+
+def pick_plan(*args):
+    n_rep, n_table = lax.axis_size("rep"), lax.axis_size("table")
+    cold_table, hot_table, relations, head_row, neg_ids = args[0], args[2], args[4], args[6], args[9]
+    if fits_kernel(
+        n_rep,
+        n_table,
+        cold_table.shape[0],
+        hot_table.shape[0],
+        head_row.shape[0],
+        neg_ids.shape[1],
+        cold_table.shape[1],
+        relations.shape[0],
+    ):
+        return per_device_kernel(*args)
+    return per_device(*args)
 
 
 def solution(mesh):
@@ -120,5 +566,5 @@
     )
     out_specs = (P("table", None), P("table"), P("table", None), P("table"))
     return jax.shard_map(
-        per_device, mesh=mesh, in_specs=in_specs, out_specs=out_specs, check_vma=False
-    )
+        pick_plan, mesh=mesh, in_specs=in_specs, out_specs=out_specs, check_vma=False
+    )

time: 256 us -> 122 us (0.48)
  waiting for transfers between devices: 117 us -> 0 us
  Pallas kernels: 0 us -> 104 us
  other arithmetic: 39.1 us -> 1.43 us
  blocking collectives: 28.9 us -> 0 us
  local copies, waits for them, and re-layouts: 43.2 us -> 15.8 us
  between operations: 14 us -> 0.68 us
  starting transfers between devices: 5.9 us -> 0 us
  matrix products: 5.16 us -> 0 us
    pallas_call x0 -> x1, Pallas kernels: none -> 104 us  [per_device_kernel(): pl.pallas_call(functools.partial(edge_kernel, (n_rep, n_table)), out_shap...]
    psum x1 -> x0, waiting for transfers between devices: 81.6 us -> none  [per_device(): cold_total, hot_total = lax.psum((cold_grad, hot_share), 'rep')]
    reduce_scatter x2 -> x0, waiting for transfers between devices: 35.5 us -> none  [the longest x1 35.5 us: per_device(): lax.psum_scatter(hot_grad, 'table', scatter_dimension=0, tiled=True)]
    all_gather x2 -> x0, blocking collectives: 28.9 us -> none  [the longest x1 16.3 us: per_device(): lax.all_gather(hot_bf, 'table', axis=0, tiled=True)]
    scatter-add x3 -> x0, other arithmetic: 19.5 us -> none  [the longest x1 9.36 us: per_device(): jnp.zeros((hot_all.shape[0], feature_width), jnp.float32).at[tail_ids]]
    gather x6 -> x0, local copies, waits for them, and re-layouts: 19.3 us -> none  [the longest x2 7.28 us: per_device(): cold_bf[row_ids]]
    sub x3 -> x0, other arithmetic: 5.92 us -> none  [the longest x2 3.42 us: adagrad(): weights - learn_rate * grad / jnp.sqrt(new_state)[:, None]]
    all_to_all x1 -> x0, starting transfers between devices: 5.64 us -> none  [per_device(): lax.all_to_all(packed.reshape(4, n_table, capacity), 'table', split_axis=...]
  transfers between devices with their start and end apart: 4 -> 0, of which waited for: 2 -> 0; matrix products, arithmetic and copies ran while one was open for 13% -> 0% of each run, Pallas kernels for 0% -> 0%
where the time goes in v1:
time: 122 us
  Pallas kernels  104 us (85%)
  local copies, waits for them, and re-layouts  15.8 us (13%)
  other arithmetic  1.43 us (1%)
    pallas_call x1, Pallas kernels, per_device_kernel(): pl.pallas_call(functools.partial(edge_kernel, (n_rep, n_table)), out_shap...  104 us
    unnamed x14, local copies, waits for them, and re-layouts  11.3 us

profile of v1, /device:TPU:9, one launch (start us, length us, event | category | flops | bytes accessed | tf_op | source)
XLA Modules:
  0.0 122.0 jit_solution(8138435583137241940)
XLA Ops:
  0.6 0.0 copy-start
  0.6 1.4 %copy.28.nid_ref = s32[8,1]{1,0:T(8,128)} copy(s32[8,1]{0,1:T(1,128)} %bitcast.11) | data formatting | bytes 64 | tf_op jit(solution)/shard_map/reshape | solution.py:532
  2.1 1.4 %copy.25.hstate_ref = f32[128,1]{1,0:T(8,128)} copy(f32[128,1]{0,1:T(1,128)} %bitcast.10) | data formatting | bytes 1024 | tf_op jit(solution)/shard_map/broadcast_in_dim | solution.py:526
  3.5 1.8 %copy.24.hot_ref = f32[128,400]{1,0:T(8,128)} copy(f32[128,400]{0,1:T(8,128)} %param.12) | data formatting | bytes 409600 | tf_op args[2]
  5.2 1.6 %copy.27.owner_ref = s32[512,1]{1,0:T(8,128)} copy(s32[512,1]{0,1:T(1,128)} %param.15) | data formatting | bytes 4096 | tf_op args[5]
  6.8 1.7 %copy.23.cstate_ref = f32[1024,1]{1,0:T(8,128)} copy(f32[1024,1]{0,1:T(1,128)} %bitcast.6) | data formatting | bytes 8192 | tf_op jit(solution)/shard_map/broadcast_in_dim | solution.py:524
  8.5 2.5 %copy.26.rel_ref = f32[512,400]{1,0:T(8,128)} copy(f32[512,400]{0,1:T(8,128)} %param.14) | data formatting | bytes 1638400 | tf_op args[4]
  11.0 0.0 copy-done
  11.0 1.8 %copy.22.cold_ref = f32[1024,400]{1,0:T(8,128)} copy(f32[1024,400]{0,1:T(8,128)S(1)} %copy-done) | data formatting | bytes 3276800 | tf_op args[0]
  12.8 104.1 %edge_window.1 = (f32[1024,400]{1,0:T(8,128)}, f32[1024,1]{1,0:T(8,128)}, f32[128,400]{1,0:T(8,128)}, f32[128,1]{1,0:T(8,128)}) custom-call(f32[1024,400]{1,0:T(8,128)} %copy.22.cold_ref, f32[1024,1]{1,0:T(8,128)} %copy.23.cstate_ref, f32[128,400]{1,0:T(8,128)} %copy.24.hot_ref, f32[128,1]{1,0:T(8,128)} %copy.25.hstate_ref, f32[512,400]{1,0:T(8,128)} %copy.26.rel_ref, ...), custom_call_target="tpu_custom_call" | custom-call | tf_op jit(solution)/shard_map/edge_window/pallas_call | solution.py:474
  116.9 0.0 copy-start.3
  116.9 0.0 copy-start.1
  116.9 0.0 copy-start.2
  116.9 2.8 %copy.29 = f32[1024,400]{0,1:T(8,128)} copy(f32[1024,400]{1,0:T(8,128)} %get-tuple-element.16) | data formatting | bytes 3276800
  119.7 0.0 copy-done.3
  119.7 0.6 reduce.1
  120.3 0.0 copy-done.1
  120.3 0.8 reduce
  121.1 0.0 copy-done.2
  121.1 0.8 copy.30
Async XLA Ops:
  0.6 10.3 %copy-start = (f32[1024,400]{0,1:T(8,128)S(1)}, f32[1024,400]{0,1:T(8,128)}, u32[]{:S(2)}) copy-start(f32[1024,400]{0,1:T(8,128)} %param.10) | copy-start | bytes 4915204
  116.9 2.8 %copy-start.3 = (f32[128,1]{1,0:T(8,128)S(1)}, f32[128,1]{1,0:T(8,128)}, u32[]{:S(2)}) copy-start(f32[128,1]{1,0:T(8,128)} %get-tuple-element.11) | copy-start | bytes 1540
  116.9 3.5 %copy-start.1 = (f32[1024,1]{1,0:T(8,128)S(1)}, f32[1024,1]{1,0:T(8,128)}, u32[]{:S(2)}) copy-start(f32[1024,1]{1,0:T(8,128)} %get-tuple-element.9) | copy-start | bytes 12292
  116.9 4.3 %copy-start.2 = (f32[128,400]{1,0:T(8,128)S(1)}, f32[128,400]{1,0:T(8,128)}, u32[]{:S(2)}) copy-start(f32[128,400]{1,0:T(8,128)} %get-tuple-element.18) | copy-start | bytes 614404

commit v2 on v1

--- a/solution.py
+++ b/solution.py
@@ -118,11 +118,11 @@
     return (
         all(s & (s - 1) == 0 for s in sizes)
         and 2 * edges // n_table == 128
-        and n_table % 2 == 0
+        and n_table % 4 == 0
         and quarter % 16 == 0
         and quarter <= 256
         and neg_dev == 8
-        and cold_rows % 128 == 0
+        and cold_rows % 256 == 0
         and cold_rows <= 4096
         and width % 2 == 0
         and width <= 512
@@ -316,12 +316,12 @@
         r_re, r_im, v_re, v_im = r[:, :padw], r[:, padw:], v[:, :padw], v[:, padw:]
         return jnp.concatenate([r_re * v_re + r_im * v_im, r_re * v_im - r_im * v_re], axis=1)
 
-    chunk = 256
+    chunk = 512
     per = n_table * 128 // chunk
 
     def edges_of(q, own):
         def body(c, carry):
-            f = jnp.concatenate([ids[q, 2 * c], ids[q, 2 * c + 1]], axis=1)
+            f = jnp.concatenate([ids[q, 4 * c + i] for i in range(4)], axis=1)
             g = f.T.astype(i32)
             f = f.astype(i32)
             row_row = f[0:1] * 32 + f[1:2]
@@ -416,13 +416,19 @@
         new_state = state + jnp.sum(grad * grad, axis=1, keepdims=True) / width
         return weights - learn_rate * close(grad) / jnp.sqrt(new_state), new_state
 
+    def column(v):
+        return jnp.broadcast_to(v, (8, v.shape[1])).T[:, :1]
+
+    def line(v):
+        return jnp.broadcast_to(v, (v.shape[0], 128)).T[:1]
+
     neg_total = negfin[...].reshape(n_rep * 8, full)
     neg_hi = neg_total.astype(bf16)
     neg_rest = neg_total - neg_hi.astype(f32)
     neg_mid = neg_rest.astype(bf16)
     neg_lo = (neg_rest - neg_mid.astype(f32)).astype(bf16)
-    neg_col = nidall[...].reshape(n_rep * 8, 128).astype(i32)
-    block = 128
+    neg_col = nidall[...].reshape(n_rep * 8, 128).astype(i32)[:, :1]
+    block = 256
 
     def finish(b, carry):
         start = pl.multiple_of(b * block, block)
@@ -434,18 +440,18 @@
         put = hot_one(lax.broadcasted_iota(i32, (n_rep * 8, block), 1) + start == neg_col)
         grad = grad + (dot(put, neg_hi, 0, 0) + dot(put, neg_mid, 0, 0) + dot(put, neg_lo, 0, 0))
         at = pl.ds(start, block)
-        table, state = step(cold_ref[at, :], cstate_ref[at, :], grad)
+        table, state = step(cold_ref[at, :], column(cstate_ref[:, at]), grad)
         cold_out[at, :] = table
-        cstate_out[at, :] = state
+        cstate_out[:, at] = line(state)
         return carry
 
     lax.fori_loop(0, rows_c // block, finish, 0)
 
     for c in fifth:
         c.wait()
-    table, state = step(hot_ref[...], hstate_ref[...], hotfin[...].reshape(rows_h, full))
+    table, state = step(hot_ref[...], column(hstate_ref[...]), hotfin[...].reshape(rows_h, full))
     hot_out[...] = table
-    hstate_out[...] = state
+    hstate_out[...] = line(state)
 
 
 def per_device_kernel(
@@ -466,7 +472,7 @@
     edges = head_row.shape[0]
     rel_count = relations.shape[0]
     quarter = rows_h // n_rep
-    full, chunk = 512, 256
+    full, chunk = 512, 512
     per = n_table * 128 // chunk
     f32, bf16 = jnp.float32, jnp.bfloat16
     dma = pltpu.SemaphoreType.DMA
@@ -475,9 +481,9 @@
         functools.partial(edge_kernel, (n_rep, n_table)),
         out_shape=[
             jax.ShapeDtypeStruct((rows_c, width), f32),
-            jax.ShapeDtypeStruct((rows_c, 1), f32),
+            jax.ShapeDtypeStruct((1, rows_c), f32),
             jax.ShapeDtypeStruct((rows_h, width), f32),
-            jax.ShapeDtypeStruct((rows_h, 1), f32),
+            jax.ShapeDtypeStruct((1, rows_h), f32),
         ],
         in_specs=[vmem] * 10,
         out_specs=[vmem] * 4,
@@ -521,9 +527,9 @@
         name="edge_window",
     )(
         cold_table,
-        cold_state[:, None],
+        cold_state[None, :],
         hot_table,
-        hot_state[:, None],
+        hot_state[None, :],
         relations,
         head_owner,
         head_row[None, :],
@@ -531,7 +537,7 @@
         edge_tail[None, :],
         neg_ids.reshape(-1, 1),
     )
-    return (outs[0], outs[1][:, 0], outs[2], outs[3][:, 0])
+    return (outs[0], outs[1][0], outs[2], outs[3][0])
 
 
 def pick_plan(*args):

time: 122 us -> 116 us (0.951)
  Pallas kernels: 104 us -> 101 us
  local copies, waits for them, and re-layouts: 15.8 us -> 13.8 us
  other arithmetic: 1.43 us -> 0 us
    pallas_call x1, Pallas kernels: 104 us -> 101 us  [per_device_kernel(): pl.pallas_call(functools.partial(edge_kernel, (n_rep, n_table)), out_shap...]
    broadcast_in_dim x2 -> x0, local copies, waits for them, and re-layouts: 3.09 us -> none  [the longest x1 1.71 us: per_device_kernel(): cold_state[:, None]]
    pallas_call x2 -> x0, other arithmetic: 1.43 us -> none  [per_device_kernel(): pl.pallas_call(functools.partial(edge_kernel, (n_rep, n_table)), out_shap...]
    unnamed x14 -> x16, local copies, waits for them, and re-layouts: 11.3 us -> 12.3 us
where the time goes in v2:
time: 116 us; the launch traced here: 115 us
  Pallas kernels  101 us (87%)
  local copies, waits for them, and re-layouts  13.8 us (12%)
    pallas_call x1, Pallas kernels, per_device_kernel(): pl.pallas_call(functools.partial(edge_kernel, (n_rep, n_table)), out_shap...  101 us
    unnamed x16, local copies, waits for them, and re-layouts  12.3 us

profile of v2, /device:TPU:9, one launch (start us, length us, event | category | flops | bytes accessed | tf_op | source)
XLA Modules:
  0.0 115.3 jit_solution(18053821075419880250)
XLA Ops:
  0.6 0.0 copy-start
  0.6 1.4 %copy.18.nid_ref = s32[8,1]{1,0:T(8,128)} copy(s32[8,1]{0,1:T(1,128)} %bitcast.14) | data formatting | bytes 64 | tf_op jit(solution)/shard_map/reshape | solution.py:538
  2.1 1.8 %copy.15.hot_ref = f32[128,400]{1,0:T(8,128)} copy(f32[128,400]{0,1:T(8,128)} %param.12) | data formatting | bytes 409600 | tf_op args[2]
  3.8 1.6 %copy.17.owner_ref = s32[512,1]{1,0:T(8,128)} copy(s32[512,1]{0,1:T(1,128)} %param.15) | data formatting | bytes 4096 | tf_op args[5]
  5.4 2.5 %copy.16.rel_ref = f32[512,400]{1,0:T(8,128)} copy(f32[512,400]{0,1:T(8,128)} %param.14) | data formatting | bytes 1638400 | tf_op args[4]
  7.9 0.0 copy-done
  7.9 1.8 %copy.14.cold_ref = f32[1024,400]{1,0:T(8,128)} copy(f32[1024,400]{0,1:T(8,128)S(1)} %copy-done) | data formatting | bytes 3276800 | tf_op args[0]
  9.7 100.9 %edge_window.1 = (f32[1024,400]{1,0:T(8,128)}, f32[1,1024]{1,0:T(1,128)}, f32[128,400]{1,0:T(8,128)}, f32[1,128]{1,0:T(1,128)}) custom-call(f32[1024,400]{1,0:T(8,128)} %copy.14.cold_ref, f32[1,1024]{1,0:T(1,128)} %bitcast.9, f32[128,400]{1,0:T(8,128)} %copy.15.hot_ref, f32[1,128]{1,0:T(1,128)} %bitcast.13, f32[512,400]{1,0:T(8,128)} %copy.16.rel_ref, ...), custom_call_target="tpu_custom_call" | custom-call | tf_op jit(solution)/shard_map/edge_window/pallas_call | solution.py:480
  110.6 0.0 copy-start.1
  110.6 0.0 copy-start.2
  110.6 0.0 copy-start.3
  110.6 2.8 %copy.19 = f32[1024,400]{0,1:T(8,128)} copy(f32[1024,400]{1,0:T(8,128)} %get-tuple-element.12) | data formatting | bytes 3276800
  113.4 0.0 copy-done.1
  113.4 0.8 copy.20
  114.2 0.0 copy-done.2
  114.2 0.6 copy.23
  114.8 0.0 copy-done.3
  114.8 0.5 copy.24
Async XLA Ops:
  0.6 7.2 %copy-start = (f32[1024,400]{0,1:T(8,128)S(1)}, f32[1024,400]{0,1:T(8,128)}, u32[]{:S(2)}) copy-start(f32[1024,400]{0,1:T(8,128)} %param.10) | copy-start | bytes 4915204
  110.6 2.8 %copy-start.1 = (f32[128,400]{1,0:T(8,128)S(1)}, f32[128,400]{1,0:T(8,128)}, u32[]{:S(2)}) copy-start(f32[128,400]{1,0:T(8,128)} %get-tuple-element.14) | copy-start | bytes 614404
  110.6 3.6 %copy-start.2 = (f32[1,1024]{1,0:T(1,128)S(1)}, f32[1,1024]{1,0:T(1,128)}, u32[]{:S(2)}) copy-start(f32[1,1024]{1,0:T(1,128)} %get-tuple-element.9) | copy-start | bytes 12292
  110.6 4.2 %copy-start.3 = (f32[1,128]{1,0:T(1,128)S(1)}, f32[1,128]{1,0:T(1,128)}, u32[]{:S(2)}) copy-start(f32[1,128]{1,0:T(1,128)} %get-tuple-element.11) | copy-start | bytes 1540
